TPU v7x, 256 devices: a whole 4x4x8 slice. The times are simulated.
256 devices in a mesh: wave: 64 (over x, z, core), lev: 4 (over y).
Axes of the slice: x: 4, y: 4, z: 8, core: 2. Of those that a mesh axis runs over, the one named last changes fastest.
Arguments:
- fourier: bfloat16 [2, 2, 72, 1280, 640], P(None, None, 'lev', 'wave'), may hold values from -6 to 6
- lat_order: int32 [1280], replicated, may hold values from 0 to 1279, each once
- wave_order: int32 [640], replicated, may hold values from 0 to 639, as said below
- pattern: int32 [64, 64], replicated, may hold values from 0 to 1, as said below
- legendre: bfloat16 [640, 640, 640], P('wave'), may hold values from -0.25 to 0.25
- lat_weight: float32 [640], replicated, may hold values from 0.2 to 1.8
- hydrostatic_thermal_link: float32 [72, 72], replicated, may hold values from -0.75 to 0.75
- evec: float32 [72, 72], replicated, may hold values from -0.75 to 0.75
- einv: float32 [72, 72], replicated, may hold values from -0.75 to 0.75
- spread_to_heat_link: float32 [72, 72], replicated, may hold values from -0.75 to 0.75
- modes: float32 [72], replicated, may hold values from 0.5 to 50
Outputs:
- new_fourier: bfloat16 [2, 2, 72, 1280, 640], P(None, None, 'lev', 'wave')
Inputs may be any that keep to these rules, and one draw needn't show every extreme that they name: `wave_order`: each wavenumber appears once; positions 2i and 2i+1 hold a wavenumber p and 639-p. pattern[i, j] is 1 where j >= i and 0 where j < i - 1.
All inputs are finite; a program needn't handle non-finite values.
Results may differ from a plain program's by a relative error of at most 0.0061.
Values may be sent and summed in bfloat16 or wider, within the bound.
No kernel may reach another device: no remote copies, remote signals or barrier semaphores. Data moves between devices by JAX's collectives and lax.ppermute only.
A program may use at most 128 MiB of HBM per device.

v0:
```python
import jax
import jax.numpy as jnp
from jax import lax
from jax.experimental import pallas as pl
from jax.experimental.pallas import tpu as pltpu
from jax.sharding import PartitionSpec as P

RQ, R5 = 4, 5
CUTS = 2
X = 72
XP = 80
FL = 36
FLP = 40
LANES = 384
NT = (((1,), (1,)), ((), ()))
TN = (((0,), (0,)), ((), ()))
NN = (((1,), (0,)), ((), ()))
F32 = jnp.float32
BF16 = jnp.bfloat16


def dot(a, b, dims):
    return lax.dot_general(a, b, dims, preferred_element_type=F32)


def params():
    return pltpu.CompilerParams(vmem_limit_bytes=26 * 1024 * 1024)


def put_rows(scr, start, size, stride, values):
    width = scr.shape[2]
    for t in range(scr.shape[0]):
        scr[t, pl.ds(start, size, stride=stride), :] = values[:, t * width : (t + 1) * width]


def get_rows(scr, start, size, stride):
    tiles = [scr[t, pl.ds(start, size, stride=stride), :] for t in range(scr.shape[0])]
    return jnp.concatenate(tiles, axis=1)


def put_block(scr, block):
    width = scr.shape[2]
    for t in range(scr.shape[0]):
        part = block[:, :, t * width : (t + 1) * width].astype(F32)
        scr[t] = part.reshape(scr.shape[1:])


def get_block(scr, out_ref):
    width = scr.shape[2]
    for t in range(scr.shape[0]):
        part = scr[t].reshape(out_ref.shape[:2] + (width,))
        out_ref[:, :, t * width : (t + 1) * width] = part.astype(BF16)


def tiles_of(size):
    return (size // 128, 128) if size % 128 == 0 else (1, size)


def h_block(lat_half):
    return 128 if lat_half % 128 == 0 else lat_half


def wave_matrix(wave_ref, m_local):
    count = wave_ref.shape[1]
    peers = count // m_local
    row = lax.broadcasted_iota(jnp.int32, (count, count), 0)
    ids = lax.broadcasted_iota(jnp.int32, (count, count), 1)
    slot = lax.rem(row, peers) * m_local + lax.div(row, peers)
    waves = wave_ref[...].astype(F32)
    held = jnp.sum(jnp.where(ids == slot, waves, 0.0), axis=1, keepdims=True)
    return jnp.where(held == ids.astype(F32), 1.0, 0.0).astype(BF16)


def fill_lat_matrix(lat_ref, ot_scr):
    lat_count = ot_scr.shape[0]
    half = lat_count // 2
    hb = h_block(half)
    lats = lat_ref[...]
    for block in range(half // hb):
        ids = lax.broadcasted_iota(jnp.int32, (hb, lat_count), 0) + block * hb
        north = jnp.where(lats == ids, 1.0, 0.0).astype(BF16)
        south = jnp.where(lats == lat_count - 1 - ids, 1.0, 0.0).astype(BF16)
        ot_scr[2 * block * hb : (2 * block + 1) * hb, :] = north
        ot_scr[(2 * block + 1) * hb : (2 * block + 2) * hb, :] = south


def lat_kernel(lat_ref, out_ref):
    fill_lat_matrix(lat_ref, out_ref)


def select_kernel(wave_ref, x_hbm, out_hbm, x_buf, z_scr, scr, out_buf, in_sem, out_sem):
    count, rows = out_buf.shape[0], out_buf.shape[1]
    m_local = rows // RQ
    loads = []
    for rq in range(RQ):
        part = pl.ds(rq * R5, R5)
        loads.append(pltpu.make_async_copy(x_hbm.at[:, part], x_buf.at[:, part], in_sem.at[rq]))
        loads[-1].start()
    onehot = wave_matrix(wave_ref, m_local)
    z_scr[R5 * X :, :] = jnp.zeros((LANES - R5 * X, z_scr.shape[1]), BF16)
    for rq in range(RQ):
        loads[rq].wait()
        for r5 in range(R5):
            piece = x_buf[:, rq * R5 + r5].reshape(X, z_scr.shape[1])
            z_scr[r5 * X : (r5 + 1) * X, :] = piece
        got = dot(onehot, z_scr[...], NT)
        for kk in range(m_local):
            put_rows(scr, kk * RQ + rq, count, rows, got[kk * count : (kk + 1) * count])
    step = count // CUTS
    width = scr.shape[2]
    stores = []
    for cut in range(CUTS):
        part = pl.ds(cut * step, step)
        for t in range(scr.shape[0]):
            lanes = pl.ds(t * width, width)
            piece = scr[t, pl.ds(cut * step * rows, step * rows), :].reshape(step, rows, width)
            out_buf[part, :, lanes] = piece.astype(BF16)
        stores.append(pltpu.make_async_copy(out_buf.at[part], out_hbm.at[part], out_sem.at[cut]))
        stores[-1].start()
    for store in stores:
        store.wait()


def forward_kernel(r_ref, ot_scr, weight_ref, even_ref, odd_ref, leg_ref, out_hbm, scr, rt_scr, sa_scr, sp_scr, out_ref, out_sem):
    count, rows = r_ref.shape[0], r_ref.shape[1]
    m_local = rows // RQ
    half = ot_scr.shape[0] // 2
    hb = h_block(half)
    span = RQ * count

    put_block(scr, r_ref[...])
    for kk in range(m_local):
        part = jnp.concatenate(
            [get_rows(scr, kk * RQ + rq, count, rows) for rq in range(RQ)], axis=0
        )
        turned = part.T
        for r5 in range(R5):
            rt_scr[kk, :X, r5 * span : (r5 + 1) * span] = turned[r5 * X : (r5 + 1) * X].astype(BF16)
    lhs = rt_scr[...].reshape(m_local * XP, 2 * half)
    for block in range(half // hb):
        both = dot(lhs, ot_scr[2 * block * hb : (2 * block + 2) * hb, :], NT)
        north, south = both[:, :hb], both[:, hb:]
        weight = weight_ref[:, block * hb : (block + 1) * hb]
        sym = ((north + south) * weight).astype(BF16)
        anti = ((north - south) * weight).astype(BF16)
        sa_scr[:, :XP, block * hb : (block + 1) * hb] = sym.reshape(m_local, XP, hb)
        sa_scr[:, XP:, block * hb : (block + 1) * hb] = anti.reshape(m_local, XP, hb)

    stores = []
    for kk in range(m_local):
        pair, k2 = kk // 2, kk % 2
        terms = dot(sa_scr[kk], leg_ref[kk], NT)
        put_rows(sp_scr, 0, X, 1, terms[:X] * even_ref[kk] + terms[XP : XP + X] * odd_ref[kk])
        for c in range(2):
            picked = get_rows(sp_scr, c, FL, 2)
            picked = jnp.concatenate([picked, jnp.zeros((FLP - FL, picked.shape[1]), F32)], axis=0)
            out_ref[pair, 2 * k2 + c] = picked.astype(BF16)
        if k2 == 1:
            stores.append(
                pltpu.make_async_copy(out_ref.at[pair], out_hbm.at[:, pair], out_sem.at[pair])
            )
            stores[-1].start()
    for store in stores:
        store.wait()


def split(values):
    high = values.astype(BF16)
    return high, (values - high.astype(F32)).astype(BF16)


def solve_kernel(r_ref, first_ref, second_ref, modes_ref, keep_ref, out_ref):
    waves = r_ref.shape[3]
    first_high, first_low = split(first_ref[...])
    second_high, second_low = split(second_ref[...])
    ids = lax.broadcasted_iota(jnp.int32, (1, waves), 1)
    factor = (ids * (ids + 1)).astype(F32) / float(waves * (waves + 1))
    scale = 1.0 / (1.0 + factor * modes_ref[...])
    for pair in range(r_ref.shape[1]):
        state = r_ref[:, pair].astype(F32).reshape(4 * FLP, waves)
        state_low = state.astype(BF16)
        both = dot(first_high, state_low, NN) + dot(first_low, state_low, NN)
        modal = (both[:X] + factor * both[X:]) * scale
        modal_high, modal_low = split(modal)
        new = (
            dot(second_high, modal_high, NN)
            + dot(second_high, modal_low, NN)
            + dot(second_low, modal_high, NN)
        )
        new = new + keep_ref[...] * state
        out_ref[:, pair] = new.reshape(4, FLP, waves).astype(BF16)


def inverse_kernel(v_ref, ot_scr, live_ref, signed_ref, leg_ref, out_ref, scr, ns_scr, v_scr, b_scr):
    count, rows = out_ref.shape[0], out_ref.shape[1]
    m_local = rows // RQ
    half = ot_scr.shape[0] // 2
    hb = h_block(half)
    span = RQ * count
    v_scr[...] = jnp.zeros_like(v_scr)
    for kk in range(m_local):
        pair, k2 = kk // 2, kk % 2
        for c in range(2):
            put_rows(v_scr, c, FL, 2, v_ref[2 * k2 + c, pair].astype(F32)[:FL])
        values = get_rows(v_scr, 0, XP, 1)
        lhs = jnp.concatenate([values * live_ref[kk], values * signed_ref[kk]], axis=0).astype(BF16)
        grid = dot(lhs, leg_ref[kk], NN).astype(BF16)
        for block in range(half // hb):
            piece = grid[:, block * hb : (block + 1) * hb]
            ns_scr[kk, :, 2 * block * hb : (2 * block + 1) * hb] = piece[:XP]
            ns_scr[kk, :, (2 * block + 1) * hb : (2 * block + 2) * hb] = piece[XP:]
    lhs = ns_scr[...].reshape(m_local * XP, 2 * half)
    for r5 in range(R5):
        band = dot(lhs, ot_scr[:, r5 * span : (r5 + 1) * span], NN)
        b_scr[:, r5 * X : (r5 + 1) * X, :] = band.reshape(m_local, XP, span)[:, :X]
    for kk in range(m_local):
        turned = b_scr[kk].T
        for rq in range(RQ):
            put_rows(scr, kk * RQ + rq, count, rows, turned[rq * count : (rq + 1) * count])
    get_block(scr, out_ref)


def restore_kernel(wave_ref, r_ref, out_hbm, scr, out_buf, out_sem):
    count, rows = r_ref.shape[0], r_ref.shape[1]
    m_local = rows // RQ
    waves = wave_ref.shape[1]
    onehot = wave_matrix(wave_ref, m_local)
    put_block(scr, r_ref[...])
    stores = []
    for rq in range(RQ):
        part = jnp.concatenate(
            [get_rows(scr, kk * RQ + rq, count, rows) for kk in range(m_local)], axis=0
        )
        got = dot(part.astype(BF16), onehot, TN).astype(BF16)
        for r5 in range(R5):
            piece = got[r5 * X : (r5 + 1) * X].reshape(FL, 2, waves)
            out_buf[:, rq * R5 + r5] = piece
        part = pl.ds(rq * R5, R5)
        stores.append(pltpu.make_async_copy(out_buf.at[:, part], out_hbm.at[:, part], out_sem.at[rq]))
        stores[-1].start()
    for store in stores:
        store.wait()


def local(
    fourier,
    lat_order,
    wave_order,
    pattern,
    legendre,
    lat_weight,
    hydrostatic_thermal_link,
    evec,
    einv,
    spread_to_heat_link,
    modes,
):
    m_local, waves, lat_half = legendre.shape
    lat_count = 2 * lat_half
    count = waves // m_local
    rows = m_local * RQ
    pairs = m_local // 2
    block_count = pattern.shape[0]
    block_width = waves // block_count
    lev_local = fourier.shape[2]
    high = lax.Precision.HIGHEST

    wave_row = wave_order.reshape(1, waves)
    lat_row = lat_order.reshape(count, RQ, R5).transpose(2, 1, 0).reshape(1, lat_count)
    weight_row = lat_weight.reshape(1, lat_half)

    my_waves = lax.dynamic_slice_in_dim(wave_order, lax.axis_index("wave") * m_local, m_local)
    degrees = jnp.arange(waves, dtype=jnp.int32)
    parity_even = (degrees[None, :] - my_waves[:, None]) % 2 == 0
    owner_rows = (
        my_waves[:, None] // block_width == jnp.arange(block_count, dtype=jnp.int32)[None, :]
    ).astype(F32)
    live_rows = jnp.dot(owner_rows, pattern.astype(F32), precision=high)
    live = jnp.repeat(live_rows, block_width, axis=1)
    even = jnp.where(parity_even, live, 0.0)[:, None, :]
    odd = jnp.where(parity_even, 0.0, live)[:, None, :]
    signed = jnp.where(parity_even, live, -live)[:, None, :]
    live = live[:, None, :]

    einv_link = jnp.dot(einv, hydrostatic_thermal_link, precision=high)
    heat_evec = jnp.dot(spread_to_heat_link, evec, precision=high)
    lev_count = LEVS = einv.shape[0] // lev_local
    first = jnp.stack([einv, einv_link]).reshape(2, X, lev_count, lev_local)
    eye2 = jnp.eye(2, dtype=F32)
    first = (first.transpose(0, 1, 2, 3)[:, :, :, None, :] * eye2[:, None, None, :, None])
    first = first.reshape(2 * X, lev_count, 2 * lev_local)
    first = jnp.pad(first, ((0, 0), (0, 0), (0, FLP - FL))).reshape(2 * X, lev_count * FLP)
    second = jnp.stack([evec, -heat_evec]).reshape(2, lev_count, lev_local, X)
    second = second.transpose(1, 0, 2, 3).reshape(lev_count, 2 * lev_local, X)
    second = jnp.pad(second, ((0, 0), (0, FLP - FL), (0, 0))).reshape(lev_count * FLP, X)
    place = jnp.arange(lev_count * FLP, dtype=jnp.int32) % FLP
    keep = ((place >= lev_local) & (place < 2 * lev_local)).astype(F32)[:, None]

    vmem = pl.BlockSpec(memory_space=pltpu.VMEM)
    anywhere = pl.BlockSpec(memory_space=pltpu.HBM)
    block_scratch = pltpu.VMEM((LANES // 128, count * rows, 128), F32)
    block_shape = jax.ShapeDtypeStruct((count, rows, LANES), BF16)
    rowed = (2 * lev_local, RQ * R5, 2, waves)
    picked = pl.pallas_call(
        select_kernel,
        in_specs=[vmem, anywhere],
        out_specs=anywhere,
        out_shape=block_shape,
        scratch_shapes=[
            pltpu.VMEM(rowed, BF16),
            pltpu.VMEM((LANES, waves), BF16),
            block_scratch,
            pltpu.VMEM(block_shape.shape, BF16),
            pltpu.SemaphoreType.DMA((RQ,)),
            pltpu.SemaphoreType.DMA((CUTS,)),
        ],
        compiler_params=params(),
        name="select_waves",
    )(wave_row, fourier.transpose(0, 2, 3, 1, 4).reshape(rowed))
    arrived = lax.all_to_all(picked, "wave", split_axis=0, concat_axis=0, tiled=True)
    lat_matrix = pl.pallas_call(
        lat_kernel,
        in_specs=[vmem],
        out_specs=vmem,
        out_shape=jax.ShapeDtypeStruct((lat_count, lat_count), BF16),
        compiler_params=params(),
        name="lat_matrix",
    )(lat_row)

    spec_shape = jax.ShapeDtypeStruct((4, pairs, FLP, waves), BF16)
    lane_tiles, lane_width = tiles_of(waves)
    spectra = pl.pallas_call(
        forward_kernel,
        in_specs=[vmem] * 6,
        out_specs=anywhere,
        out_shape=spec_shape,
        scratch_shapes=[
            block_scratch,
            pltpu.VMEM((m_local, XP, lat_count), BF16),
            pltpu.VMEM((m_local, 2 * XP, lat_half), BF16),
            pltpu.VMEM((lane_tiles, X, lane_width), F32),
            pltpu.VMEM((pairs, 4, FLP, waves), BF16),
            pltpu.SemaphoreType.DMA((pairs,)),
        ],
        compiler_params=params(),
        name="forward_legendre",
    )(arrived, lat_matrix, weight_row, even, odd, legendre)
    shifted = lax.all_to_all(spectra, "lev", split_axis=0, concat_axis=0, tiled=True)
    solved = pl.pallas_call(
        solve_kernel,
        in_specs=[vmem] * 5,
        out_specs=vmem,
        out_shape=spec_shape,
        compiler_params=params(),
        name="solve_levels",
    )(shifted, first, second, modes[:, None], keep)
    back = lax.all_to_all(solved, "lev", split_axis=0, concat_axis=0, tiled=True)
    banded = pl.pallas_call(
        inverse_kernel,
        in_specs=[vmem] * 5,
        out_specs=vmem,
        out_shape=block_shape,
        scratch_shapes=[
            block_scratch,
            pltpu.VMEM((m_local, XP, lat_count), BF16),
            pltpu.VMEM((lane_tiles, XP, lane_width), F32),
            pltpu.VMEM((m_local, LANES, RQ * count), F32),
        ],
        compiler_params=params(),
        name="inverse_legendre",
    )(back, lat_matrix, live, signed, legendre)
    returned = lax.all_to_all(banded, "wave", split_axis=0, concat_axis=0, tiled=True)
    restored = pl.pallas_call(
        restore_kernel,
        in_specs=[vmem] * 2,
        out_specs=anywhere,
        out_shape=jax.ShapeDtypeStruct(rowed, BF16),
        scratch_shapes=[
            block_scratch,
            pltpu.VMEM(rowed, BF16),
            pltpu.SemaphoreType.DMA((RQ,)),
        ],
        compiler_params=params(),
        name="restore_waves",
    )(wave_row, returned)
    restored = restored.reshape(2, lev_local, RQ * R5, 2, waves)
    return restored.transpose(0, 3, 1, 2, 4)


def solution(mesh):
    placed = (
        P(None, None, "lev", "wave", None),
        P(),
        P(),
        P(),
        P("wave", None, None),
        P(),
        P(),
        P(),
        P(),
        P(),
        P(),
    )
    return jax.shard_map(
        local,
        mesh=mesh,
        in_specs=placed,
        out_specs=P(None, None, "lev", "wave", None),
        check_vma=False,
    )
```

profile of v0, /device:TPU:1, one launch (start us, length us, event | category | flops | bytes accessed | tf_op | source)
XLA Modules:
  0.0 191.4 jit_solution(7530304078318987153)
XLA Ops:
  0.0 0.0 copy-start
  0.0 0.7 reshape.233.wave_ref
  0.7 0.0 copy-start.4
  0.7 1.5 copy-done.4
  2.2 5.2 %select_waves.1 = bf16[64,40,384]{2,1,0:T(8,128)(2,1)} custom-call(s32[1,640]{1,0:T(1,128)S(1)} %reshape.233.wave_ref, bf16[36,20,2,640]{3,2,1,0:T(2,128)(2,1)S(1)} %bitcast.27), custom_call_target="tpu_custom_call" | custom-call | tf_op jit(solution)/shard_map/select_waves/pallas_call | solution.py:304
  7.4 0.0 copy-start.12
  7.4 13.2 %all-to-all-start = ((bf16[64,40,384]{2,1,0:T(8,128)(2,1)}), bf16[64,40,384]{2,1,0:T(8,128)(2,1)}, u32[]{:S(2)}, u32[]{:S(2)}) async-start(bf16[64,40,384]{2,1,0:T(8,128)(2,1)} %select_waves.1), calls=%async_computation | async-start | bytes 3932160 | tf_op jit(solution)/shard_map/all_to_all | solution.py:320
  20.5 0.0 copy-start.13
  20.6 0.0 copy-start.15
  20.6 0.0 copy-done.12
  20.6 0.2 reshape.235
  20.8 0.1 copy.28
  20.9 0.1 reshape.236.lat_ref
  21.0 0.0 copy-start.11
  21.0 0.6 lat_matrix.1.ot_scr
  21.6 0.0 copy-done.13
  21.6 0.8 and_select_fusion.1
  22.4 0.0 copy-done.15
  22.4 0.2 fusion.7
  22.6 0.9 broadcast_in_dim.10
  23.5 1.2 reshape.243.live_ref
  24.7 0.0 copy-done.11
  24.7 0.0 copy-start.6
  24.7 0.1 copy.31
  24.8 0.0 copy-done
  24.8 0.3 fusion.12
  25.1 0.1 copy.33
  25.2 0.8 mul.28
  26.1 0.8 negate_select_fusion
  26.8 41.9 %all-to-all-done.r_ref = bf16[64,40,384]{2,1,0:T(8,128)(2,1)} async-done(((bf16[64,40,384]{2,1,0:T(8,128)(2,1)}), bf16[64,40,384]{2,1,0:T(8,128)(2,1)}, u32[]{:S(2)}, u32[]{:S(2)}) %all-to-all-start) | async-done | bytes 1966112 | tf_op jit(solution)/shard_map/all_to_all | solution.py:320
  68.7 0.0 copy-start.1
  68.7 3.3 %copy-done.1 = bf16[10,640,640]{2,1,0:T(8,128)(2,1)S(1)} copy-done((bf16[10,640,640]{2,1,0:T(8,128)(2,1)S(1)}, bf16[10,640,640]{2,1,0:T(8,128)(2,1)}, u32[]{:S(2)}) %copy-start.1) | copy-done | bytes 8192024
  72.0 9.4 %forward_legendre.1 = bf16[4,5,40,640]{3,2,1,0:T(8,128)(2,1)S(1)} custom-call(bf16[64,40,384]{2,1,0:T(8,128)(2,1)} %all-to-all-done.r_ref, bf16[1280,1280]{1,0:T(8,128)(2,1)S(1)} %lat_matrix.1.ot_scr, f32[1,640]{1,0:T(1,128)S(1)} %reshape.237.weight_ref, f32[10,1,640]{2,1,0:T(1,128)S(1)} %get-tuple-element.9.even_ref, ...), custom_call_target="tpu_custom_call" | custom-call | tf_op jit(solution)/shard_map/forward_legendre/pallas_call | solution.py:332
  81.5 0.0 copy-done.6
  81.5 0.0 copy-start.3
  81.5 0.9 copy-done.3
  82.4 0.0 copy-start.10
  82.4 0.0 copy-start.14
  82.4 4.5 %all-to-all-start.1 = ((bf16[4,5,40,640]{3,2,1,0:T(8,128)(2,1)}), bf16[4,5,40,640]{3,2,1,0:T(8,128)(2,1)}, u32[]{:S(2)}, u32[]{:S(2)}) async-start(bf16[4,5,40,640]{3,2,1,0:T(8,128)(2,1)} %copy-done.3), calls=%async_computation.1 | async-start | bytes 2048000 | tf_op jit(solution)/shard_map/all_to_all | solution.py:348
  87.0 0.7 mul.29
  87.7 0.9 mul.30
  88.6 0.0 copy-done.10
  88.6 0.7 pad.8.clone
  89.3 1.0 copy.38.first_ref
  90.4 0.8 stack.21
  91.1 1.0 convolution_negate_fusion
  92.1 0.6 stack.22
  92.7 0.8 maximum_bitcast_fusion.1
  93.6 0.0 copy-done.14
  93.6 0.7 copy.39.modes_ref
  94.3 0.7 fusion.5.keep_ref
  95.0 6.4 %all-to-all-done.1.r_ref = bf16[4,5,40,640]{3,2,1,0:T(8,128)(2,1)} async-done(((bf16[4,5,40,640]{3,2,1,0:T(8,128)(2,1)}), bf16[4,5,40,640]{3,2,1,0:T(8,128)(2,1)}, u32[]{:S(2)}, u32[]{:S(2)}) %all-to-all-start.1) | async-done | bytes 1024032 | tf_op jit(solution)/shard_map/all_to_all | solution.py:348
  101.4 0.0 copy-start.5
  101.4 0.9 copy-done.5
  102.3 0.0 copy-start.8
  102.3 0.8 copy-done.8
  103.0 3.3 %solve_levels.1 = bf16[4,5,40,640]{3,2,1,0:T(8,128)(2,1)S(1)} custom-call(bf16[4,5,40,640]{3,2,1,0:T(8,128)(2,1)} %all-to-all-done.1.r_ref, f32[144,160]{1,0:T(8,128)S(1)} %copy.38.first_ref, f32[160,72]{1,0:T(8,128)S(1)} %bitcast.28, f32[72,1]{1,0:T(8,128)S(1)} %copy-done.8, f32[160,1]{1,0:T(8,128)S(1)} %copy-done.5), custom_call_target="tpu_custom_call" | custom-call | tf_op jit(solution)/shard_map/solve_levels/pallas_call | solution.py:349
  106.4 15.8 %all_to_all.20.v_ref = bf16[4,5,40,640]{3,2,1,0:T(8,128)(2,1)S(1)} all-to-all(bf16[4,5,40,640]{3,2,1,0:T(8,128)(2,1)S(1)} %solve_levels.1), channel_id=1, replica_groups=mesh['wave'=64,'lev'=4] {'lev'}, dimensions={0} | all-to-all | bytes 2048000 | tf_op jit(solution)/shard_map/all_to_all | solution.py:357
  122.2 0.0 copy-done.7
  122.2 0.0 copy-done.9
  122.2 3.3 %copy-done.2 = bf16[10,640,640]{2,1,0:T(8,128)(2,1)S(1)} copy-done((bf16[10,640,640]{2,1,0:T(8,128)(2,1)S(1)}, bf16[10,640,640]{2,1,0:T(8,128)(2,1)}, u32[]{:S(2)}) %copy-start.2) | copy-done | bytes 8192024
  125.5 5.5 %inverse_legendre.1 = bf16[64,40,384]{2,1,0:T(8,128)(2,1)S(1)} custom-call(bf16[4,5,40,640]{3,2,1,0:T(8,128)(2,1)S(1)} %all_to_all.20.v_ref, bf16[1280,1280]{1,0:T(8,128)(2,1)S(1)} %lat_matrix.1.ot_scr, f32[10,1,640]{2,1,0:T(1,128)S(1)} %copy-done.7, f32[10,1,640]{2,1,0:T(1,128)S(1)} %copy-done.9, bf16[10,640,640]{2,1,0:T(8,128)(2,1)S(1)} %copy-done.2), custom_call_target="tpu_custom_call" | custom-call | tf_op jit(solution)/shard_map/inverse_legendre/pallas_call | solution.py:358
  131.0 56.8 %all_to_all.21.r_ref = bf16[64,40,384]{2,1,0:T(8,128)(2,1)S(1)} all-to-all(bf16[64,40,384]{2,1,0:T(8,128)(2,1)S(1)} %inverse_legendre.1), channel_id=1, replica_groups=mesh['wave'=64,'lev'=4] {'wave'}, dimensions={0} | all-to-all | bytes 3932160 | tf_op jit(solution)/shard_map/all_to_all | solution.py:372
  187.8 3.4 %restore_waves.1 = bf16[36,20,2,640]{3,2,1,0:T(2,128)(2,1)} custom-call(s32[1,640]{1,0:T(1,128)S(1)} %reshape.233.wave_ref, bf16[64,40,384]{2,1,0:T(8,128)(2,1)S(1)} %all_to_all.21.r_ref), custom_call_target="tpu_custom_call" | custom-call | tf_op jit(solution)/shard_map/restore_waves/pallas_call | solution.py:373
  (14 shorter events, 0.2 us)
Async XLA Ops:
  0.0 24.8 %copy-start = (f32[72,72]{1,0:T(8,128)S(1)}, f32[72,72]{1,0:T(8,128)}, u32[]{:S(2)}) copy-start(f32[72,72]{1,0:T(8,128)} %param.17) | copy-start | bytes 62212
  0.7 1.5 copy-start.4
  7.4 13.2 %copy-start.12 = (s32[1280]{0:T(1024)S(1)}, s32[1280]{0:T(1024)}, u32[]{:S(2)}) copy-start(s32[1280]{0:T(1024)} %param.12) | copy-start | bytes 15364
  7.4 61.3 %all-to-all-start = ((bf16[64,40,384]{2,1,0:T(8,128)(2,1)}), bf16[64,40,384]{2,1,0:T(8,128)(2,1)}, u32[]{:S(2)}, u32[]{:S(2)}) async-start(bf16[64,40,384]{2,1,0:T(8,128)(2,1)} %select_waves.1), calls=%async_computation | async-start | bytes 3932160 | tf_op jit(solution)/shard_map/all_to_all | solution.py:320
  20.5 1.1 copy-start.13
  20.6 1.8 copy-start.15
  21.0 3.7 %copy-start.11 = (f32[72,72]{1,0:T(8,128)S(1)}, f32[72,72]{1,0:T(8,128)}, u32[]{:S(2)}) copy-start(f32[72,72]{1,0:T(8,128)} %param.19) | copy-start | bytes 62212
  24.7 56.7 %copy-start.6 = (f32[10,1,640]{2,1,0:T(1,128)}, f32[10,1,640]{2,1,0:T(1,128)S(1)}, u32[]{:S(2)}) copy-start(f32[10,1,640]{2,1,0:T(1,128)S(1)} %reshape.243.live_ref) | copy-start | bytes 76804
  68.7 3.3 %copy-start.1 = (bf16[10,640,640]{2,1,0:T(8,128)(2,1)S(1)}, bf16[10,640,640]{2,1,0:T(8,128)(2,1)}, u32[]{:S(2)}) copy-start(bf16[10,640,640]{2,1,0:T(8,128)(2,1)} %leg_ref.3) | copy-start | bytes 24576004
  81.5 1.0 copy-start.3
  82.4 6.1 %copy-start.10 = (f32[144,4,36]{0,1,2:T(4,128)S(1)}, f32[144,4,36]{0,1,2:T(4,128)}, u32[]{:S(2)}) copy-start(f32[144,4,36]{0,1,2:T(4,128)} %mul.28) | copy-start | bytes 248836
  82.4 11.2 %copy-start.14 = (f32[72]{0:T(128)S(1)}, f32[72]{0:T(128)}, u32[]{:S(2)}) copy-start(f32[72]{0:T(128)} %param.21) | copy-start | bytes 868
  82.4 19.0 %all-to-all-start.1 = ((bf16[4,5,40,640]{3,2,1,0:T(8,128)(2,1)}), bf16[4,5,40,640]{3,2,1,0:T(8,128)(2,1)}, u32[]{:S(2)}, u32[]{:S(2)}) async-start(bf16[4,5,40,640]{3,2,1,0:T(8,128)(2,1)} %copy-done.3), calls=%async_computation.1 | async-start | bytes 2048000 | tf_op jit(solution)/shard_map/all_to_all | solution.py:348
  101.4 0.9 copy-start.5
  102.3 0.8 copy-start.8
  103.0 19.1 %copy-start.7 = (f32[10,1,640]{2,1,0:T(1,128)S(1)}, f32[10,1,640]{2,1,0:T(1,128)}, u32[]{:S(2)}) copy-start(f32[10,1,640]{2,1,0:T(1,128)} %copy-done.6) | copy-start | bytes 76804
  103.0 19.1 %copy-start.9 = (f32[10,1,640]{2,1,0:T(1,128)S(1)}, f32[10,1,640]{2,1,0:T(1,128)}, u32[]{:S(2)}) copy-start(f32[10,1,640]{2,1,0:T(1,128)} %get-tuple-element.7.signed_ref) | copy-start | bytes 76804
  122.2 3.3 %copy-start.2 = (bf16[10,640,640]{2,1,0:T(8,128)(2,1)S(1)}, bf16[10,640,640]{2,1,0:T(8,128)(2,1)}, u32[]{:S(2)}) copy-start(bf16[10,640,640]{2,1,0:T(8,128)(2,1)} %leg_ref.3) | copy-start | bytes 24576004
where the time goes:
time: 192 us; the launch traced here: 191 us
  blocking collectives  72.5 us (38%)
  waiting for transfers between devices  48.3 us (25%)
  Pallas kernels  27.4 us (14%)
  local copies, waits for them, and re-layouts  20.5 us (11%)
  starting transfers between devices  17.7 us (9%)
  other arithmetic  3.09 us (2%)
    all_to_all x1, blocking collectives, local(): lax.all_to_all(banded, 'wave', split_axis=0, concat_axis=0, tiled=True)  56.8 us
    all_to_all x1, waiting for transfers between devices, local(): lax.all_to_all(picked, 'wave', split_axis=0, concat_axis=0, tiled=True)  41.9 us
    all_to_all x1, blocking collectives, local(): lax.all_to_all(solved, 'lev', split_axis=0, concat_axis=0, tiled=True)  15.8 us
    all_to_all x1, starting transfers between devices, local(): lax.all_to_all(picked, 'wave', split_axis=0, concat_axis=0, tiled=True)  13.2 us
    unnamed x35, local copies, waits for them, and re-layouts  10.9 us
    pallas_call x1, Pallas kernels, local(): pl.pallas_call(forward_kernel, in_specs=[vmem] * 6, out_specs=anywhere, o...  9.42 us
    all_to_all x1, waiting for transfers between devices, local(): lax.all_to_all(spectra, 'lev', split_axis=0, concat_axis=0, tiled=True)  6.38 us
    pallas_call x1, Pallas kernels, local(): pl.pallas_call(inverse_kernel, in_specs=[vmem] * 5, out_specs=vmem, out_s...  5.5 us
  transfers between devices with their start and end apart: 2, of which 2 were waited for; matrix products, arithmetic and copies ran while one was open for 7% of the time, Pallas kernels for 0%

commit v1 on v0

--- a/solution.py
+++ b/solution.py
@@ -1,3 +1,5 @@
+import functools
+
 import jax
 import jax.numpy as jnp
 from jax import lax
@@ -11,6 +13,8 @@
 XP = 80
 FL = 36
 FLP = 40
+LEV = 4
+GAP = 128
 LANES = 384
 NT = (((1,), (1,)), ((), ()))
 TN = (((0,), (0,)), ((), ()))
@@ -23,8 +27,8 @@
     return lax.dot_general(a, b, dims, preferred_element_type=F32)
 
 
-def params():
-    return pltpu.CompilerParams(vmem_limit_bytes=26 * 1024 * 1024)
+def params(mebibytes=50):
+    return pltpu.CompilerParams(vmem_limit_bytes=mebibytes * 1024 * 1024)
 
 
 def put_rows(scr, start, size, stride, values):
@@ -61,12 +65,12 @@
 
 
 def wave_matrix(wave_ref, m_local):
-    count = wave_ref.shape[1]
+    count = wave_ref.shape[0]
     peers = count // m_local
     row = lax.broadcasted_iota(jnp.int32, (count, count), 0)
     ids = lax.broadcasted_iota(jnp.int32, (count, count), 1)
     slot = lax.rem(row, peers) * m_local + lax.div(row, peers)
-    waves = wave_ref[...].astype(F32)
+    waves = wave_ref[...].reshape(1, count).astype(F32)
     held = jnp.sum(jnp.where(ids == slot, waves, 0.0), axis=1, keepdims=True)
     return jnp.where(held == ids.astype(F32), 1.0, 0.0).astype(BF16)
 
@@ -121,13 +125,25 @@
         store.wait()
 
 
-def forward_kernel(r_ref, ot_scr, weight_ref, even_ref, odd_ref, leg_ref, out_hbm, scr, rt_scr, sa_scr, sp_scr, out_ref, out_sem):
+def fetch_legendre(leg_hbm, leg_buf, leg_sem):
+    loads = []
+    for kk in range(leg_buf.shape[0]):
+        loads.append(pltpu.make_async_copy(leg_hbm.at[kk], leg_buf.at[kk], leg_sem.at[kk]))
+        loads[-1].start()
+    return loads
+
+
+def forward_kernel(
+    place_ref, r_ref, ot_scr, weight_ref, even_ref, odd_ref, leg_hbm,
+    out0, out1, out2, out3, scr, rt_scr, sa_scr, sp_scr, out_scr, leg_buf, leg_sem,
+):
     count, rows = r_ref.shape[0], r_ref.shape[1]
     m_local = rows // RQ
     half = ot_scr.shape[0] // 2
     hb = h_block(half)
     span = RQ * count
-
+    slots = 2 * out_scr.shape[3]
+    loads = fetch_legendre(leg_hbm, leg_buf, leg_sem)
     put_block(scr, r_ref[...])
     for kk in range(m_local):
         part = jnp.concatenate(
@@ -146,22 +162,23 @@
         sa_scr[:, :XP, block * hb : (block + 1) * hb] = sym.reshape(m_local, XP, hb)
         sa_scr[:, XP:, block * hb : (block + 1) * hb] = anti.reshape(m_local, XP, hb)
 
-    stores = []
-    for kk in range(m_local):
-        pair, k2 = kk // 2, kk % 2
-        terms = dot(sa_scr[kk], leg_ref[kk], NT)
-        put_rows(sp_scr, 0, X, 1, terms[:X] * even_ref[kk] + terms[XP : XP + X] * odd_ref[kk])
+    for pair in range(m_local // 2):
+        packed = jnp.zeros((X, slots), F32)
+        for kk in (2 * pair, 2 * pair + 1):
+            loads[kk].wait()
+            terms = dot(sa_scr[kk], leg_buf[kk], NT)
+            picked = terms[:X] * even_ref[kk] + terms[XP : XP + X] * odd_ref[kk]
+            picked = jnp.concatenate([picked, jnp.zeros((X, GAP), F32)], axis=1)
+            packed = packed + pltpu.roll(picked, place_ref[kk], 1)
+        put_rows(sp_scr, 0, X, 1, packed)
         for c in range(2):
-            picked = get_rows(sp_scr, c, FL, 2)
-            picked = jnp.concatenate([picked, jnp.zeros((FLP - FL, picked.shape[1]), F32)], axis=0)
-            out_ref[pair, 2 * k2 + c] = picked.astype(BF16)
-        if k2 == 1:
-            stores.append(
-                pltpu.make_async_copy(out_ref.at[pair], out_hbm.at[:, pair], out_sem.at[pair])
-            )
-            stores[-1].start()
-    for store in stores:
-        store.wait()
+            part = get_rows(sp_scr, c, FL, 2)
+            part = jnp.concatenate([part, jnp.zeros((FLP - FL, slots), F32)], axis=0).astype(BF16)
+            out_scr[2 * c, pair] = part[:, : slots // 2]
+            out_scr[2 * c + 1, pair] = part[:, slots // 2 :]
+    me = place_ref[2 * m_local]
+    for shift, out in enumerate((out0, out1, out2, out3)):
+        out[...] = out_scr[lax.rem(me + shift, LEV)]
 
 
 def split(values):
@@ -169,18 +186,23 @@
     return high, (values - high.astype(F32)).astype(BF16)
 
 
-def solve_kernel(r_ref, first_ref, second_ref, modes_ref, keep_ref, out_ref):
-    waves = r_ref.shape[3]
+def solve_kernel(
+    place_ref, r0, r1, r2, r3, first_ref, second_ref, modes_ref, keep_ref,
+    out0, out1, out2, out3, *, waves, m_local,
+):
+    pairs, _, width = r0.shape
     first_high, first_low = split(first_ref[...])
     second_high, second_low = split(second_ref[...])
-    ids = lax.broadcasted_iota(jnp.int32, (1, waves), 1)
-    factor = (ids * (ids + 1)).astype(F32) / float(waves * (waves + 1))
-    scale = 1.0 / (1.0 + factor * modes_ref[...])
-    for pair in range(r_ref.shape[1]):
-        state = r_ref[:, pair].astype(F32).reshape(4 * FLP, waves)
+    side = lax.rem(place_ref[2 * m_local], 2)
+    slot = lax.broadcasted_iota(jnp.int32, (1, width), 1) + side * width
+    for pair in range(pairs):
+        lower = slot + place_ref[m_local + pairs + pair]
+        degree = jnp.where(slot >= place_ref[m_local + pair], slot - GAP, lower)
+        factor = (degree * (degree + 1)).astype(F32) / float(waves * (waves + 1))
+        state = jnp.concatenate([r[pair].astype(F32) for r in (r0, r1, r2, r3)], axis=0)
         state_low = state.astype(BF16)
         both = dot(first_high, state_low, NN) + dot(first_low, state_low, NN)
-        modal = (both[:X] + factor * both[X:]) * scale
+        modal = (both[:X] + factor * both[X:]) / (1.0 + factor * modes_ref[...])
         modal_high, modal_low = split(modal)
         new = (
             dot(second_high, modal_high, NN)
@@ -188,23 +210,36 @@
             + dot(second_low, modal_high, NN)
         )
         new = new + keep_ref[...] * state
-        out_ref[:, pair] = new.reshape(4, FLP, waves).astype(BF16)
-
-
-def inverse_kernel(v_ref, ot_scr, live_ref, signed_ref, leg_ref, out_ref, scr, ns_scr, v_scr, b_scr):
+        for shift, out in enumerate((out0, out1, out2, out3)):
+            out[pair] = new[shift * FLP : (shift + 1) * FLP].astype(BF16)
+
+
+def inverse_kernel(
+    place_ref, v0, v1, v2, v3, ot_scr, live_ref, signed_ref, leg_hbm,
+    out_ref, scr, ns_scr, in_scr, v_scr, b_scr, leg_buf, leg_sem,
+):
     count, rows = out_ref.shape[0], out_ref.shape[1]
     m_local = rows // RQ
     half = ot_scr.shape[0] // 2
     hb = h_block(half)
     span = RQ * count
+    waves = live_ref.shape[2]
+    loads = fetch_legendre(leg_hbm, leg_buf, leg_sem)
+    me = place_ref[2 * m_local]
+    for shift, value in enumerate((v0, v1, v2, v3)):
+        in_scr[lax.rem(me + shift, LEV)] = value[...]
     v_scr[...] = jnp.zeros_like(v_scr)
     for kk in range(m_local):
         pair, k2 = kk // 2, kk % 2
-        for c in range(2):
-            put_rows(v_scr, c, FL, 2, v_ref[2 * k2 + c, pair].astype(F32)[:FL])
-        values = get_rows(v_scr, 0, XP, 1)
+        if k2 == 0:
+            for c in range(2):
+                part = jnp.concatenate([in_scr[2 * c, pair], in_scr[2 * c + 1, pair]], axis=1)
+                put_rows(v_scr, c, FL, 2, part.astype(F32)[:FL])
+            packed = get_rows(v_scr, 0, XP, 1)
+        values = pltpu.roll(packed, waves + GAP - place_ref[kk], 1)[:, :waves]
         lhs = jnp.concatenate([values * live_ref[kk], values * signed_ref[kk]], axis=0).astype(BF16)
-        grid = dot(lhs, leg_ref[kk], NN).astype(BF16)
+        loads[kk].wait()
+        grid = dot(lhs, leg_buf[kk], NN).astype(BF16)
         for block in range(half // hb):
             piece = grid[:, block * hb : (block + 1) * hb]
             ns_scr[kk, :, 2 * block * hb : (2 * block + 1) * hb] = piece[:XP]
@@ -223,7 +258,7 @@
 def restore_kernel(wave_ref, r_ref, out_hbm, scr, out_buf, out_sem):
     count, rows = r_ref.shape[0], r_ref.shape[1]
     m_local = rows // RQ
-    waves = wave_ref.shape[1]
+    waves = wave_ref.shape[0]
     onehot = wave_matrix(wave_ref, m_local)
     put_block(scr, r_ref[...])
     stores = []
@@ -240,6 +275,14 @@
         stores[-1].start()
     for store in stores:
         store.wait()
+
+
+def turn(blocks, sign):
+    sent = list(blocks)
+    for shift in (2, 1, 3):
+        route = [(i, (i + sign * shift) % LEV) for i in range(LEV)]
+        sent[shift] = lax.ppermute(blocks[shift], "lev", route)
+    return sent
 
 
 def local(
@@ -263,9 +306,9 @@
     block_count = pattern.shape[0]
     block_width = waves // block_count
     lev_local = fourier.shape[2]
+    lev_count = LEV
     high = lax.Precision.HIGHEST
 
-    wave_row = wave_order.reshape(1, waves)
     lat_row = lat_order.reshape(count, RQ, R5).transpose(2, 1, 0).reshape(1, lat_count)
     weight_row = lat_weight.reshape(1, lat_half)
 
@@ -281,18 +324,33 @@
     odd = jnp.where(parity_even, 0.0, live)[:, None, :]
     signed = jnp.where(parity_even, live, -live)[:, None, :]
     live = live[:, None, :]
+    lev_index = lax.axis_index("lev")
+    edge = (my_waves // block_width - 1) * block_width
+    low = my_waves < waves // 2
+    slots = waves + GAP
+    offset = jnp.where(low, GAP, slots - edge)
+    edges, lows = edge.reshape(pairs, 2), low.reshape(pairs, 2)
+    limit = jnp.sum(jnp.where(lows, edges, 0), axis=1) + GAP // 2 + block_width
+    upper = jnp.sum(jnp.where(lows, 0, edges), axis=1)
+    places = jnp.concatenate([offset, limit, upper, lev_index[None]]).astype(jnp.int32)
+
+    def from_me(blocks, axis):
+        back = jnp.flip(blocks, axis)
+        twice = jnp.concatenate([back, back], axis)
+        return lax.dynamic_slice_in_dim(twice, lev_count - 1 - lev_index, lev_count, axis)
 
     einv_link = jnp.dot(einv, hydrostatic_thermal_link, precision=high)
     heat_evec = jnp.dot(spread_to_heat_link, evec, precision=high)
-    lev_count = LEVS = einv.shape[0] // lev_local
     first = jnp.stack([einv, einv_link]).reshape(2, X, lev_count, lev_local)
     eye2 = jnp.eye(2, dtype=F32)
     first = (first.transpose(0, 1, 2, 3)[:, :, :, None, :] * eye2[:, None, None, :, None])
     first = first.reshape(2 * X, lev_count, 2 * lev_local)
-    first = jnp.pad(first, ((0, 0), (0, 0), (0, FLP - FL))).reshape(2 * X, lev_count * FLP)
+    first = jnp.pad(first, ((0, 0), (0, 0), (0, FLP - FL)))
+    first = from_me(first, 1).reshape(2 * X, lev_count * FLP)
     second = jnp.stack([evec, -heat_evec]).reshape(2, lev_count, lev_local, X)
     second = second.transpose(1, 0, 2, 3).reshape(lev_count, 2 * lev_local, X)
-    second = jnp.pad(second, ((0, 0), (0, FLP - FL), (0, 0))).reshape(lev_count * FLP, X)
+    second = jnp.pad(second, ((0, 0), (0, FLP - FL), (0, 0)))
+    second = from_me(second, 0).reshape(lev_count * FLP, X)
     place = jnp.arange(lev_count * FLP, dtype=jnp.int32) % FLP
     keep = ((place >= lev_local) & (place < 2 * lev_local)).astype(F32)[:, None]
 
@@ -314,9 +372,9 @@
             pltpu.SemaphoreType.DMA((RQ,)),
             pltpu.SemaphoreType.DMA((CUTS,)),
         ],
-        compiler_params=params(),
+        compiler_params=params(60),
         name="select_waves",
-    )(wave_row, fourier.transpose(0, 2, 3, 1, 4).reshape(rowed))
+    )(wave_order, fourier.transpose(0, 2, 3, 1, 4).reshape(rowed))
     arrived = lax.all_to_all(picked, "wave", split_axis=0, concat_axis=0, tiled=True)
     lat_matrix = pl.pallas_call(
         lat_kernel,
@@ -327,48 +385,62 @@
         name="lat_matrix",
     )(lat_row)
 
-    spec_shape = jax.ShapeDtypeStruct((4, pairs, FLP, waves), BF16)
-    lane_tiles, lane_width = tiles_of(waves)
+    modes_col = modes[:, None]
+    lat_matrix, weight_row, even, odd, live, signed, first, second, modes_col, keep, places = (
+        lax.optimization_barrier(
+            (lat_matrix, weight_row, even, odd, live, signed, first, second, modes_col, keep, places)
+        )
+    )
+
+    smem = pl.BlockSpec(memory_space=pltpu.SMEM)
+    spec_shape = jax.ShapeDtypeStruct((pairs, FLP, slots // 2), BF16)
+    lane_tiles, lane_width = tiles_of(slots)
+    leg_scratch = [
+        pltpu.VMEM(legendre.shape, BF16),
+        pltpu.SemaphoreType.DMA((m_local,)),
+    ]
     spectra = pl.pallas_call(
         forward_kernel,
-        in_specs=[vmem] * 6,
-        out_specs=anywhere,
-        out_shape=spec_shape,
+        in_specs=[smem] + [vmem] * 5 + [anywhere],
+        out_specs=[vmem] * LEV,
+        out_shape=[spec_shape] * LEV,
         scratch_shapes=[
             block_scratch,
             pltpu.VMEM((m_local, XP, lat_count), BF16),
             pltpu.VMEM((m_local, 2 * XP, lat_half), BF16),
             pltpu.VMEM((lane_tiles, X, lane_width), F32),
-            pltpu.VMEM((pairs, 4, FLP, waves), BF16),
-            pltpu.SemaphoreType.DMA((pairs,)),
-        ],
+            pltpu.VMEM((LEV,) + spec_shape.shape, BF16),
+        ]
+        + leg_scratch,
         compiler_params=params(),
         name="forward_legendre",
-    )(arrived, lat_matrix, weight_row, even, odd, legendre)
-    shifted = lax.all_to_all(spectra, "lev", split_axis=0, concat_axis=0, tiled=True)
+    )(places, arrived, lat_matrix, weight_row, even, odd, legendre)
+    shifted = turn(spectra, 1)
     solved = pl.pallas_call(
-        solve_kernel,
-        in_specs=[vmem] * 5,
-        out_specs=vmem,
-        out_shape=spec_shape,
+        functools.partial(solve_kernel, waves=waves, m_local=m_local),
+        in_specs=[smem] + [vmem] * (LEV + 4),
+        out_specs=[vmem] * LEV,
+        out_shape=[spec_shape] * LEV,
         compiler_params=params(),
         name="solve_levels",
-    )(shifted, first, second, modes[:, None], keep)
-    back = lax.all_to_all(solved, "lev", split_axis=0, concat_axis=0, tiled=True)
+    )(places, *shifted, first, second, modes_col, keep)
+    back = turn(solved, -1)
     banded = pl.pallas_call(
         inverse_kernel,
-        in_specs=[vmem] * 5,
+        in_specs=[smem] + [vmem] * (LEV + 3) + [anywhere],
         out_specs=vmem,
         out_shape=block_shape,
         scratch_shapes=[
             block_scratch,
             pltpu.VMEM((m_local, XP, lat_count), BF16),
+            pltpu.VMEM((LEV,) + spec_shape.shape, BF16),
             pltpu.VMEM((lane_tiles, XP, lane_width), F32),
             pltpu.VMEM((m_local, LANES, RQ * count), F32),
-        ],
+        ]
+        + leg_scratch,
         compiler_params=params(),
         name="inverse_legendre",
-    )(back, lat_matrix, live, signed, legendre)
+    )(places, *back, lat_matrix, live, signed, legendre)
     returned = lax.all_to_all(banded, "wave", split_axis=0, concat_axis=0, tiled=True)
     restored = pl.pallas_call(
         restore_kernel,
@@ -382,7 +454,7 @@
         ],
         compiler_params=params(),
         name="restore_waves",
-    )(wave_row, returned)
+    )(wave_order, returned)
     restored = restored.reshape(2, lev_local, RQ * R5, 2, waves)
     return restored.transpose(0, 3, 1, 2, 4)
 

time: 192 us -> 175 us (0.911)
  blocking collectives: 72.5 us -> 55 us
  local copies, waits for them, and re-layouts: 20.5 us -> 3.92 us
  waiting for transfers between devices: 48.3 us -> 57.2 us
  Pallas kernels: 27.4 us -> 34.7 us
  starting transfers between devices: 17.7 us -> 21.2 us
  other arithmetic: 3.09 us -> 0.96 us
    all_to_all x1 -> x0, blocking collectives: 15.8 us -> none  [local(): lax.all_to_all(solved, 'lev', split_axis=0, concat_axis=0, tiled=True)]
    ppermute x0 -> x6, waiting for transfers between devices: none -> 15.2 us  [turn(): sent[shift] = lax.ppermute(blocks[shift], 'lev', route)]
    unnamed x35 -> x21, local copies, waits for them, and re-layouts: 10.9 us -> 1.79 us
    ppermute x0 -> x6, starting transfers between devices: none -> 8.03 us  [turn(): sent[shift] = lax.ppermute(blocks[shift], 'lev', route)]
    all_to_all x1 -> x0, waiting for transfers between devices: 6.38 us -> none  [local(): lax.all_to_all(spectra, 'lev', split_axis=0, concat_axis=0, tiled=True)]
    pallas_call x3, Pallas kernels: 18.2 us -> 24.2 us  [the longest x1 11.8 us: local(): pl.pallas_call(forward_kernel, in_specs=[smem] + [vmem] * 5 + [anywhere],...]
    all_to_all x1 -> x0, starting transfers between devices: 4.55 us -> none  [local(): lax.all_to_all(spectra, 'lev', split_axis=0, concat_axis=0, tiled=True)]
    mul x5, local copies, waits for them, and re-layouts: 2.46 us -> 0.44 us  [local(): first.transpose(0, 1, 2, 3)[:, :, :, None, :] * eye2[:, None, None, :, None]]
  transfers between devices with their start and end apart: 2 -> 7, of which waited for: 2 -> 6; matrix products, arithmetic and copies ran while one was open for 7% -> 2% of each run, Pallas kernels for 0% -> 0%
where the time goes in v1:
time: 175 us; the launch traced here: 174 us
  waiting for transfers between devices  57.2 us (33%)
  blocking collectives  55 us (31%)
  Pallas kernels  34.7 us (20%)
  starting transfers between devices  21.2 us (12%)
  local copies, waits for them, and re-layouts  3.92 us (2%)
    all_to_all x1, blocking collectives, local(): lax.all_to_all(banded, 'wave', split_axis=0, concat_axis=0, tiled=True)  55 us
    all_to_all x1, waiting for transfers between devices, local(): lax.all_to_all(picked, 'wave', split_axis=0, concat_axis=0, tiled=True)  42.1 us
    ppermute x6, waiting for transfers between devices, turn(): sent[shift] = lax.ppermute(blocks[shift], 'lev', route)  15.2 us
    all_to_all x1, starting transfers between devices, local(): lax.all_to_all(picked, 'wave', split_axis=0, concat_axis=0, tiled=True)  13.1 us
    pallas_call x1, Pallas kernels, local(): pl.pallas_call(forward_kernel, in_specs=[smem] + [vmem] * 5 + [anywhere],...  11.8 us
    pallas_call x1, Pallas kernels, local(): pl.pallas_call(inverse_kernel, in_specs=[smem] + [vmem] * (LEV + 3) + [an...  10.3 us
    ppermute x6, starting transfers between devices, turn(): sent[shift] = lax.ppermute(blocks[shift], 'lev', route)  8.03 us
    pallas_call x1, Pallas kernels, local(): pl.pallas_call(select_kernel, in_specs=[vmem, anywhere], out_specs=anywhe...  6.45 us
  transfers between devices with their start and end apart: 7, of which 6 were waited for; matrix products, arithmetic and copies ran while one was open for 2% of the time, Pallas kernels for 0%

profile of v1, /device:TPU:1, one launch (start us, length us, event | category | flops | bytes accessed | tf_op | source)
XLA Modules:
  0.0 174.2 jit_solution(9391496357310424909)
XLA Ops:
  0.0 0.0 copy-start
  0.0 6.4 %select_waves.1 = bf16[64,40,384]{2,1,0:T(8,128)(2,1)} custom-call(s32[640]{0:T(1024)} %wave_ref.3, bf16[36,20,2,640]{3,2,1,0:T(2,128)(2,1)} %bitcast.29), custom_call_target="tpu_custom_call" | custom-call | tf_op jit(solution)/shard_map/select_waves/pallas_call | solution.py:362
  6.5 0.0 copy-start.7
  6.5 0.0 copy-start.2
  6.5 0.0 copy-start.3
  6.5 0.0 copy-start.4
  6.5 0.0 copy-start.5
  6.5 13.1 %all-to-all-start = ((bf16[64,40,384]{2,1,0:T(8,128)(2,1)}), bf16[64,40,384]{2,1,0:T(8,128)(2,1)S(1)}, u32[]{:S(2)}, u32[]{:S(2)}) async-start(bf16[64,40,384]{2,1,0:T(8,128)(2,1)} %select_waves.1), calls=%async_computation | async-start | bytes 3932160 | tf_op jit(solution)/shard_map/all_to_all | solution.py:378
  19.7 0.0 copy-done.7
  19.7 0.0 copy-done.2
  19.7 0.1 subtract_select_fusion
  19.8 0.1 select_n.112
  19.9 0.1 reduce_sum.18
  20.0 0.1 select_n.114
  20.1 0.1 reduce_sum.19
  20.2 0.1 mul.32
  20.3 0.1 mul.33
  20.4 0.0 copy-done.3
  20.4 0.1 copy.19
  20.5 0.0 copy-done
  20.5 0.3 fusion.14
  20.8 0.0 copy-done.4
  20.8 0.0 copy-start.6
  20.8 0.0 copy-done.5
  20.8 0.2 convolution_negate_fusion
  21.0 0.0 copy-start.9
  21.1 0.1 copy.21
  21.2 0.1 rev.9
  21.3 0.1 fusion.1
  21.5 0.2 mul.31
  21.7 0.3 rev.8
  22.0 0.1 fusion
  22.2 0.0 copy-done.6
  22.2 0.2 reshape.236
  22.5 0.1 copy.14
  22.6 0.1 reshape.237.lat_ref
  22.7 0.2 fusion.9
  22.9 0.2 broadcast_in_dim.20
  23.0 0.2 reshape.239
  23.2 0.6 lat_matrix.1.ot_scr
  23.8 1.7 copy-done.1
  25.5 0.1 pad_add_fusion.place_ref
  25.6 0.2 negate_select_fusion
  25.8 0.0 copy-start.8
  25.8 42.1 %all-to-all-done.r_ref = bf16[64,40,384]{2,1,0:T(8,128)(2,1)S(1)} async-done(((bf16[64,40,384]{2,1,0:T(8,128)(2,1)}), bf16[64,40,384]{2,1,0:T(8,128)(2,1)S(1)}, u32[]{:S(2)}, u32[]{:S(2)}) %all-to-all-start) | async-done | bytes 1966112 | tf_op jit(solution)/shard_map/all_to_all | solution.py:378
  67.9 11.8 %forward_legendre.1 = (bf16[5,40,384]{2,1,0:T(8,128)(2,1)S(1)}, bf16[5,40,384]{2,1,0:T(8,128)(2,1)S(1)}, bf16[5,40,384]{2,1,0:T(8,128)(2,1)S(1)}, bf16[5,40,384]{2,1,0:T(8,128)(2,1)S(1)}) custom-call(s32[21]{0:T(128)S(1)} %pad_add_fusion.place_ref, bf16[64,40,384]{2,1,0:T(8,128)(2,1)S(1)} %all-to-all-done.r_ref, bf16[1280,1280]{1,0:T(8,128)(2,1)} %copy-done.1, ...), custom_call_target="tpu_custom_call" | custom-call | tf_op jit(solution)/shard_map/forward_legendre/pallas_call | solution.py:402
  79.7 1.4 collective-permute-start
  81.1 2.6 %collective-permute-start.1 = (bf16[5,40,384]{2,1,0:T(8,128)(2,1)S(1)}, bf16[5,40,384]{2,1,0:T(8,128)(2,1)S(1)}, u32[]{:S(2)}, u32[]{:S(2)}) collective-permute-start(bf16[5,40,384]{2,1,0:T(8,128)(2,1)S(1)} %get-tuple-element.31), channel_id=1, source_target_pairs={{0,2},{1,3},{2,0},{3,1},{4,6},{5,7},{6,4},{7,5},{8,10},{9,11},{10,... | collective-permute-start | bytes 460808 | tf_op jit(solution)/shard_map/ppermute | solution.py:284
  83.7 1.1 collective-permute-start.2
  84.8 0.1 copy.26.modes_ref
  84.9 0.1 copy.25.first_ref
  85.0 1.3 collective-permute-done.r1
  86.3 4.4 %collective-permute-done.1.r2 = bf16[5,40,384]{2,1,0:T(8,128)(2,1)S(1)} collective-permute-done((bf16[5,40,384]{2,1,0:T(8,128)(2,1)S(1)}, bf16[5,40,384]{2,1,0:T(8,128)(2,1)S(1)}, u32[]{:S(2)}, u32[]{:S(2)}) %collective-permute-start.1) | collective-permute-done | bytes 153632 | tf_op jit(solution)/shard_map/ppermute | solution.py:284
  90.7 0.0 collective-permute-done.2.r3
  90.7 2.1 %solve_levels.1 = (bf16[5,40,384]{2,1,0:T(8,128)(2,1)S(1)}, bf16[5,40,384]{2,1,0:T(8,128)(2,1)S(1)}, bf16[5,40,384]{2,1,0:T(8,128)(2,1)S(1)}, bf16[5,40,384]{2,1,0:T(8,128)(2,1)S(1)}) custom-call(s32[21]{0:T(128)S(1)} %pad_add_fusion.place_ref, bf16[5,40,384]{2,1,0:T(8,128)(2,1)S(1)} %get-tuple-element.29.r0, ...), custom_call_target="tpu_custom_call" | custom-call | tf_op jit(solution)/shard_map/solve_levels/pallas_call | solution.py:419
  92.8 2.3 %collective-permute-start.3 = (bf16[5,40,384]{2,1,0:T(8,128)(2,1)S(1)}, bf16[5,40,384]{2,1,0:T(8,128)(2,1)S(1)}, u32[]{:S(2)}, u32[]{:S(2)}) collective-permute-start(bf16[5,40,384]{2,1,0:T(8,128)(2,1)S(1)} %get-tuple-element.38), channel_id=1, source_target_pairs={{0,3},{1,0},{2,1},{3,2},{4,7},{5,4},{6,5},{7,6},{8,11},{9,8},{10,9... | collective-permute-start | bytes 460808 | tf_op jit(solution)/shard_map/ppermute | solution.py:284
  95.0 0.6 collective-permute-start.4
  95.7 0.1 collective-permute-start.5
  95.8 3.3 %collective-permute-done.3.v1 = bf16[5,40,384]{2,1,0:T(8,128)(2,1)S(1)} collective-permute-done((bf16[5,40,384]{2,1,0:T(8,128)(2,1)S(1)}, bf16[5,40,384]{2,1,0:T(8,128)(2,1)S(1)}, u32[]{:S(2)}, u32[]{:S(2)}) %collective-permute-start.3) | collective-permute-done | bytes 153632 | tf_op jit(solution)/shard_map/ppermute | solution.py:284
  99.1 1.6 collective-permute-done.4.v2
  100.7 4.5 %collective-permute-done.5.v3 = bf16[5,40,384]{2,1,0:T(8,128)(2,1)S(1)} collective-permute-done((bf16[5,40,384]{2,1,0:T(8,128)(2,1)S(1)}, bf16[5,40,384]{2,1,0:T(8,128)(2,1)S(1)}, u32[]{:S(2)}, u32[]{:S(2)}) %collective-permute-start.5) | collective-permute-done | bytes 153632 | tf_op jit(solution)/shard_map/ppermute | solution.py:284
  105.3 10.3 %inverse_legendre.1 = bf16[64,40,384]{2,1,0:T(8,128)(2,1)S(1)} custom-call(s32[21]{0:T(128)S(1)} %pad_add_fusion.place_ref, bf16[5,40,384]{2,1,0:T(8,128)(2,1)S(1)} %get-tuple-element.37.v0, bf16[5,40,384]{2,1,0:T(8,128)(2,1)S(1)} %collective-permute-done.3.v1, bf16[5,40,384]{2,1,0:T(8,128)(2,1)S(1)} %collective-permute-done.4.v2, ...), custom_call_target="tpu_custom_call" | custom-call | tf_op jit(solution)/shard_map/inverse_legendre/pallas_call | solution.py:428
  115.6 55.0 %all_to_all.10.r_ref = bf16[64,40,384]{2,1,0:T(8,128)(2,1)S(1)} all-to-all(bf16[64,40,384]{2,1,0:T(8,128)(2,1)S(1)} %inverse_legendre.1), channel_id=1, replica_groups=mesh['wave'=64,'lev'=4] {'wave'}, dimensions={0} | all-to-all | bytes 3932160 | tf_op jit(solution)/shard_map/all_to_all | solution.py:444
  170.6 3.4 %restore_waves.1 = bf16[36,20,2,640]{3,2,1,0:T(2,128)(2,1)} custom-call(s32[640]{0:T(1024)S(1)} %copy-done.2, bf16[64,40,384]{2,1,0:T(8,128)(2,1)S(1)} %all_to_all.10.r_ref), custom_call_target="tpu_custom_call" | custom-call | tf_op jit(solution)/shard_map/restore_waves/pallas_call | solution.py:445
  (22 shorter events, 0.3 us)
Async XLA Ops:
  0.0 20.5 %copy-start = (f32[72,72]{1,0:T(8,128)S(1)}, f32[72,72]{1,0:T(8,128)}, u32[]{:S(2)}) copy-start(f32[72,72]{1,0:T(8,128)} %param.17) | copy-start | bytes 62212
  6.5 13.2 %copy-start.7 = (f32[640]{0:T(1024)S(1)}, f32[640]{0:T(1024)}, u32[]{:S(2)}) copy-start(f32[640]{0:T(1024)} %param.16) | copy-start | bytes 7684
  6.5 13.2 %copy-start.2 = (s32[640]{0:T(1024)S(1)}, s32[640]{0:T(1024)}, u32[]{:S(2)}) copy-start(s32[640]{0:T(1024)} %wave_ref.3) | copy-start | bytes 7684
  6.5 13.9 %copy-start.3 = (f32[72,72]{1,0:T(8,128)S(1)}, f32[72,72]{1,0:T(8,128)}, u32[]{:S(2)}) copy-start(f32[72,72]{1,0:T(8,128)} %param.19) | copy-start | bytes 62212
  6.5 14.3 %copy-start.4 = (f32[72,72]{1,0:T(8,128)S(1)}, f32[72,72]{1,0:T(8,128)}, u32[]{:S(2)}) copy-start(f32[72,72]{1,0:T(8,128)} %param.18) | copy-start | bytes 62212
  6.5 14.3 %copy-start.5 = (f32[72,72]{1,0:T(8,128)S(1)}, f32[72,72]{1,0:T(8,128)}, u32[]{:S(2)}) copy-start(f32[72,72]{1,0:T(8,128)} %param.20) | copy-start | bytes 62212
  6.5 61.4 %all-to-all-start = ((bf16[64,40,384]{2,1,0:T(8,128)(2,1)}), bf16[64,40,384]{2,1,0:T(8,128)(2,1)S(1)}, u32[]{:S(2)}, u32[]{:S(2)}) async-start(bf16[64,40,384]{2,1,0:T(8,128)(2,1)} %select_waves.1), calls=%async_computation | async-start | bytes 3932160 | tf_op jit(solution)/shard_map/all_to_all | solution.py:378
  20.8 1.4 copy-start.6
  21.0 1.6 copy-start.9
  23.8 1.7 copy-start.1
  25.8 59.0 %copy-start.8 = (f32[72]{0:T(128)S(1)}, f32[72]{0:T(128)}, u32[]{:S(2)}) copy-start(f32[72]{0:T(128)} %param.21) | copy-start | bytes 868
  79.7 6.6 %collective-permute-start = (bf16[5,40,384]{2,1,0:T(8,128)(2,1)S(1)}, bf16[5,40,384]{2,1,0:T(8,128)(2,1)S(1)}, u32[]{:S(2)}, u32[]{:S(2)}) collective-permute-start(bf16[5,40,384]{2,1,0:T(8,128)(2,1)S(1)} %get-tuple-element.30), channel_id=1, source_target_pairs={{0,1},{1,2},{2,3},{3,0},{4,5},{5,6},{6,7},{7,4},{8,9},{9,10},{10,1... | collective-permute-start | bytes 460808 | tf_op jit(solution)/shard_map/ppermute | solution.py:284
  81.1 9.6 %collective-permute-start.1 = (bf16[5,40,384]{2,1,0:T(8,128)(2,1)S(1)}, bf16[5,40,384]{2,1,0:T(8,128)(2,1)S(1)}, u32[]{:S(2)}, u32[]{:S(2)}) collective-permute-start(bf16[5,40,384]{2,1,0:T(8,128)(2,1)S(1)} %get-tuple-element.31), channel_id=1, source_target_pairs={{0,2},{1,3},{2,0},{3,1},{4,6},{5,7},{6,4},{7,5},{8,10},{9,11},{10,... | collective-permute-start | bytes 460808 | tf_op jit(solution)/shard_map/ppermute | solution.py:284
  83.7 7.0 %collective-permute-start.2 = (bf16[5,40,384]{2,1,0:T(8,128)(2,1)S(1)}, bf16[5,40,384]{2,1,0:T(8,128)(2,1)S(1)}, u32[]{:S(2)}, u32[]{:S(2)}) collective-permute-start(bf16[5,40,384]{2,1,0:T(8,128)(2,1)S(1)} %get-tuple-element.32), channel_id=1, source_target_pairs={{0,3},{1,0},{2,1},{3,2},{4,7},{5,4},{6,5},{7,6},{8,11},{9,8},{10,9... | collective-permute-start | bytes 460808 | tf_op jit(solution)/shard_map/ppermute | solution.py:284
  92.8 6.3 %collective-permute-start.3 = (bf16[5,40,384]{2,1,0:T(8,128)(2,1)S(1)}, bf16[5,40,384]{2,1,0:T(8,128)(2,1)S(1)}, u32[]{:S(2)}, u32[]{:S(2)}) collective-permute-start(bf16[5,40,384]{2,1,0:T(8,128)(2,1)S(1)} %get-tuple-element.38), channel_id=1, source_target_pairs={{0,3},{1,0},{2,1},{3,2},{4,7},{5,4},{6,5},{7,6},{8,11},{9,8},{10,9... | collective-permute-start | bytes 460808 | tf_op jit(solution)/shard_map/ppermute | solution.py:284
  95.0 5.7 %collective-permute-start.4 = (bf16[5,40,384]{2,1,0:T(8,128)(2,1)S(1)}, bf16[5,40,384]{2,1,0:T(8,128)(2,1)S(1)}, u32[]{:S(2)}, u32[]{:S(2)}) collective-permute-start(bf16[5,40,384]{2,1,0:T(8,128)(2,1)S(1)} %get-tuple-element.39), channel_id=1, source_target_pairs={{0,2},{1,3},{2,0},{3,1},{4,6},{5,7},{6,4},{7,5},{8,10},{9,11},{10,... | collective-permute-start | bytes 460808 | tf_op jit(solution)/shard_map/ppermute | solution.py:284
  95.7 9.6 %collective-permute-start.5 = (bf16[5,40,384]{2,1,0:T(8,128)(2,1)S(1)}, bf16[5,40,384]{2,1,0:T(8,128)(2,1)S(1)}, u32[]{:S(2)}, u32[]{:S(2)}) collective-permute-start(bf16[5,40,384]{2,1,0:T(8,128)(2,1)S(1)} %get-tuple-element.40), channel_id=1, source_target_pairs={{0,1},{1,2},{2,3},{3,0},{4,5},{5,6},{6,7},{7,4},{8,9},{9,10},{10,1... | collective-permute-start | bytes 460808 | tf_op jit(solution)/shard_map/ppermute | solution.py:284
